TPU v7x, 32 devices: a whole 2x2x4 slice. The times are simulated.
32 devices in a mesh: groups: 2 (over y), loop: 4 (over z), enc: 2 (over x), rep: 2 (over core).
Axes of the slice: x: 2, y: 2, z: 4, core: 2. Of those that a mesh axis runs over, the one named last changes fastest.
Arguments:
- embeddings: bfloat16 [4096, 768], P(('groups', 'loop', 'rep'), 'enc'), parts along dimension 0, may hold values from -24 to 24
- head_weight: bfloat16 [768, 768], P('enc'), may hold values from -0.21875 to 0.21875
- gp_weights: float32 [4096], P('groups'), parts along dimension 0, may hold values from -24 to 24
- counts: int32 [8], P('groups'), parts along dimension 0, may hold values from 64 to 512, as said below
Outputs:
- embed_grad: bfloat16 [4096, 768], P(('groups', 'loop', 'rep'), 'enc'), parts along dimension 0
- head_grad: float32 [1536, 768], P(('groups', 'enc')), parts along dimension 0
There are 2 independent parts, one for each index of `groups`. A program takes and returns all parts, laid end to end along the dimension named above; an argument that names none is the same for every part. Nothing has to cross between parts.
Inputs may be any that keep to these rules, and one draw needn't show every extreme that they name: `counts`: some block is full and some block holds exactly 64 valid molecules.
All inputs are finite; a program needn't handle non-finite values.
Results may differ from a plain program's by a relative error of at most 0.019.
Values may be sent and summed in bfloat16 or wider, within the bound.
A program may use at most 64 MiB of HBM per device.

v0:
```python
import jax
import jax.numpy as jnp
from jax import lax
from jax.sharding import PartitionSpec as P

EPSILON = 1e-06


def passed_along(value, axis, steps):
    count = lax.axis_size(axis)
    pairs = [(source, (source + steps) % count) for source in range(count)]
    return lax.ppermute(value, axis, pairs)


def pass_forward(piece):
    return passed_along(piece, "loop", 1)


def body(embeddings, head_weight, gp_weights, counts):
    enc_size = lax.axis_size("enc")
    rep_size = lax.axis_size("rep")
    loop_size = lax.axis_size("loop")
    share_rows = embeddings.shape[0]
    piece_rows = share_rows // enc_size
    block_rows = share_rows * rep_size
    loop_index = lax.axis_index("loop")
    enc_index = lax.axis_index("enc")
    rep_index = lax.axis_index("rep")
    rows = embeddings
    own_feats = lax.psum_scatter(
        jnp.dot(rows, head_weight, preferred_element_type=jnp.float32),
        "enc",
        scatter_dimension=0,
        tiled=True,
    ).astype(jnp.bfloat16)
    block_feats = lax.all_gather(own_feats, ("enc", "rep"), axis=0, tiled=True)
    block_norms = jnp.sum(jnp.square(block_feats.astype(jnp.float32)), axis=1)
    offsets = (
        jnp.arange(rep_size, dtype=jnp.int32)[None, :, None] * share_rows
        + jnp.arange(enc_size, dtype=jnp.int32)[:, None, None] * piece_rows
        + jnp.arange(piece_rows, dtype=jnp.int32)[None, None, :]
    ).reshape(block_rows)
    own_base = lax.dynamic_slice_in_dim(gp_weights, loop_index * block_rows, block_rows)
    block_coef = (
        own_base.reshape(rep_size, enc_size, piece_rows).transpose(1, 0, 2).reshape(block_rows)
    )
    own_count = lax.dynamic_index_in_dim(counts, loop_index, keepdims=False)
    block_coef = jnp.where(offsets < own_count, block_coef, 0.0)
    piece_start = rep_index * share_rows + enc_index * piece_rows
    piece_offsets = piece_start + jnp.arange(piece_rows, dtype=jnp.int32)

    def tile(state, piece, anchor):
        anchor_count = lax.dynamic_index_in_dim(counts, anchor, keepdims=False)
        accum, quotient_sum = state
        piece_coef = lax.dynamic_slice_in_dim(
            gp_weights, anchor * block_rows + piece_start, piece_rows
        )
        piece_coef = jnp.where(piece_offsets < anchor_count, piece_coef, 0.0)
        piece_norms = jnp.sum(jnp.square(piece.astype(jnp.float32)), axis=1)
        scores = lax.dot_general(
            piece, block_feats, (((1,), (1,)), ((), ())), preferred_element_type=jnp.float32
        )
        denom = piece_norms[:, None] + block_norms[None, :] - scores + EPSILON
        inverse = 1.0 / (denom * denom)
        pair_coef = piece_coef[:, None] * block_coef[None, :]
        pair_weight = (pair_coef * (piece_norms[:, None] + block_norms[None, :]) * inverse).astype(
            jnp.bfloat16
        )
        quotient_sum = quotient_sum + jnp.sum(pair_coef * 2.0 * scores * inverse, axis=0)
        accum = accum + lax.dot_general(
            pair_weight, piece, (((0,), (0,)), ((), ())), preferred_element_type=jnp.float32
        )
        return (accum, quotient_sum)

    start_state = (
        jnp.zeros((block_rows, block_feats.shape[1]), jnp.float32),
        jnp.zeros((block_rows,), jnp.float32),
    )
    state = tile(start_state, own_feats, loop_index)

    def forward_step(step_index, carry):
        moving, inner = carry
        moving = pass_forward(moving)
        inner = tile(inner, moving, (loop_index - step_index - 1 + loop_size) % loop_size)
        return (moving, inner)

    moving, state = lax.fori_loop(0, loop_size - 1, forward_step, (own_feats, state))
    accum, quotient_sum = state
    grad_block = accum - block_feats.astype(jnp.float32) * quotient_sum[:, None]
    own_grad = lax.psum_scatter(
        grad_block.astype(jnp.bfloat16), ("enc", "rep"), scatter_dimension=0, tiled=True
    )
    piece = lax.all_gather(own_grad, "enc", axis=0, tiled=True)
    back = lax.dot_general(
        piece, head_weight, (((1,), (1,)), ((), ())), preferred_element_type=jnp.float32
    )
    embed_part = back
    rows = embeddings
    head_part = lax.dot_general(
        rows, piece, (((0,), (0,)), ((), ())), preferred_element_type=jnp.float32
    )
    embed_part, head_part = (embed_part, head_part)
    head_grad = lax.psum(head_part, ("loop", "rep"))
    return (embed_part.astype(jnp.bfloat16), head_grad)


def solution(mesh):
    placed = (P(("groups", "loop", "rep"), "enc"), P("enc", None), P("groups"), P("groups"))
    return jax.shard_map(
        body,
        mesh=mesh,
        in_specs=placed,
        out_specs=(P(("groups", "loop", "rep"), "enc"), P(("groups", "enc"), None)),
        check_vma=False,
    )
```

profile of v0, /device:TPU:0, one launch (start us, length us, event | category | flops | bytes accessed | tf_op | source)
XLA Modules:
  0.0 170.0 jit_solution(11172648524668776611)
XLA Ops:
  7.2 1.0 copy-done
  8.2 2.2 %fusion.40 = f32[256,768]{1,0:T(8,128)} fusion(bf16[256,384]{1,0:T(8,128)(2,1)} %param.6, bf16[384,768]{1,0:T(8,128)(2,1)S(1)} %copy-done), kind=kOutput, calls=%fused_computation.56 | convolution fusion | flops 150994944 | bytes 1572864 | tf_op jit(solution)/shard_map/dot_general | solution.py:31
  10.5 0.7 dynamic_slice.37
  11.2 0.8 dynamic_slice.39
  12.0 0.8 compare_select_fusion.1
  12.8 1.5 compare_select_fusion.2
  14.2 16.8 %reduce-scatter.3.cloned.1.call-done = f32[128,768]{1,0:T(8,128)} async-done(((f32[256,768]{1,0:T(8,128)}), f32[128,768]{1,0:T(8,128)}) %reduce-scatter.3.cloned.1.call-update) | async-done | bytes 393232 | tf_op jit(solution)/shard_map/reduce_scatter | solution.py:30
  31.0 1.1 multiply_reduce_fusion.1
  32.1 8.2 %all_gather.6 = bf16[512,768]{1,0:T(8,128)(2,1)S(1)} all-gather(bf16[128,768]{1,0:T(8,128)(2,1)S(1)} %get-tuple-element.541), channel_id=1, replica_groups=mesh['groups'=2,'loop'=4,'enc'=2,'rep'=2] {'enc','rep'}, dimensions={0}, use_global_device_ids=true | all-gather | bytes 983040 | tf_op jit(solution)/shard_map/all_gather | solution.py:36
  41.5 28.3 %while.23 = (s32[]{:T(128)}, bf16[128,768]{1,0:T(8,128)(2,1)S(1)}, f32[512,768]{1,0:T(8,128)S(1)}, f32[512]{0:T(512)S(1)}, s32[]{:T(128)}, /*index=5*/s32[4]{0:T...) while((s32[]{:T(128)}, bf16[128,768]{1,0:T(8,128)(2,1)S(1)}, ...), condition=%wide.region_7.8_spmd.clone.clone, body=%wide.region_4.7_spmd.clone.clone.sunk | while | flops 203260192 | bytes 6246334 | solution.py:87
  41.5 1.5 collective-permute-start
  43.6 1.4 compare_select_fusion.4
  45.1 5.5 %collective-permute-done = bf16[128,768]{1,0:T(8,128)(2,1)S(1)} collective-permute-done((bf16[128,768]{1,0:T(8,128)(2,1)S(1)}, bf16[128,768]{1,0:T(8,128)(2,1)S(1)}, u32[]{:S(2)}, u32[]{:S(2)}) %collective-permute-start) | collective-permute-done | bytes 196640 | tf_op jit(solution)/shard_map/while/body/eval_jaxpr/ppermute | solution.py:12
  52.4 1.4 compare_select_fusion.4
  53.8 6.1 %collective-permute-done = bf16[128,768]{1,0:T(8,128)(2,1)S(1)} collective-permute-done((bf16[128,768]{1,0:T(8,128)(2,1)S(1)}, bf16[128,768]{1,0:T(8,128)(2,1)S(1)}, u32[]{:S(2)}, u32[]{:S(2)}) %collective-permute-start) | collective-permute-done | bytes 196640 | tf_op jit(solution)/shard_map/while/body/eval_jaxpr/ppermute | solution.py:12
  61.8 1.4 compare_select_fusion.4
  63.2 5.4 %collective-permute-done = bf16[128,768]{1,0:T(8,128)(2,1)S(1)} collective-permute-done((bf16[128,768]{1,0:T(8,128)(2,1)S(1)}, bf16[128,768]{1,0:T(8,128)(2,1)S(1)}, u32[]{:S(2)}, u32[]{:S(2)}) %collective-permute-start) | collective-permute-done | bytes 196640 | tf_op jit(solution)/shard_map/while/body/eval_jaxpr/ppermute | solution.py:12
  69.8 1.1 fusion.21
  71.1 20.9 %reduce-scatter.5.cloned.1.call-done = bf16[128,768]{1,0:T(8,128)(2,1)} async-done(((bf16[512,768]{1,0:T(8,128)(2,1)}), bf16[128,768]{1,0:T(8,128)(2,1)}) %reduce-scatter.5.cloned.1.call-update) | async-done | bytes 196624 | tf_op jit(solution)/shard_map/reduce_scatter | solution.py:90
  92.0 7.5 %all_gather.7 = bf16[256,768]{1,0:T(8,128)(2,1)S(1)} all-gather(bf16[128,768]{1,0:T(8,128)(2,1)} %reduce-scatter.5.cloned.1.call-done), channel_id=1, replica_groups=mesh['groups'=2,'loop'=4,'enc'=2,'rep'=2] {'enc'}, dimensions={0}, use_global_device_ids=true | all-gather | bytes 589824 | tf_op jit(solution)/shard_map/all_gather | solution.py:93
  99.5 1.4 convolution_bitcast_fusion
  100.9 1.1 convolution_convert_fusion
  102.0 58.8 %all-reduce.2.cloned.1.call-done = f32[384,768]{0,1:T(8,128)} async-done(((f32[384,768]{0,1:T(8,128)}), f32[384,768]{0,1:T(8,128)}) %all-reduce.2.cloned.1.call-update) | async-done | bytes 1179664 | tf_op jit(solution)/shard_map/psum | solution.py:103
  160.8 2.7 %copy.9 = f32[384,768]{1,0:T(8,128)} copy(f32[384,768]{0,1:T(8,128)} %all-reduce.2.cloned.1.call-done) | data formatting | bytes 2359296
  (37 shorter events, 6.8 us)
Async XLA Ops:
  7.2 1.1 copy-start
  7.2 3.3 %copy-start.2 = (s32[4]{0:T(128)S(1)}, s32[4]{0:T(128)}, u32[]{:S(2)}) copy-start(s32[4]{0:T(128)} %param.9) | copy-start | bytes 52
  7.2 23.8 %reduce-scatter.3.cloned.1.call-start = ((), (), s32[]{:S(2)}) async-start(), calls=%async_computation.2 | async-start | bytes 1179648 | tf_op jit(solution)/shard_map/reduce_scatter | solution.py:30
  10.4 81.6 %reduce-scatter.5.cloned.1.call-start = ((), (), s32[]{:S(2)}) async-start(), calls=%async_computation.3 | async-start | bytes 983040 | tf_op jit(solution)/shard_map/reduce_scatter | solution.py:90
  41.5 9.0 %collective-permute-start = (bf16[128,768]{1,0:T(8,128)(2,1)S(1)}, bf16[128,768]{1,0:T(8,128)(2,1)S(1)}, u32[]{:S(2)}, u32[]{:S(2)}) collective-permute-start(bf16[128,768]{1,0:T(8,128)(2,1)S(1)} %get-tuple-element.558), channel_id=1, source_target_pairs={{0,4},{4,8},{8,12},{12,0},{1,5},{5,9},{9,13},{13,1},{2,6},{6,10},{... | collective-permute-start | bytes 589832 | tf_op jit(solution)/shard_map/while/body/eval_jaxpr/ppermute | solution.py:12
  51.7 8.2 %collective-permute-start = (bf16[128,768]{1,0:T(8,128)(2,1)S(1)}, bf16[128,768]{1,0:T(8,128)(2,1)S(1)}, u32[]{:S(2)}, u32[]{:S(2)}) collective-permute-start(bf16[128,768]{1,0:T(8,128)(2,1)S(1)} %get-tuple-element.558), channel_id=1, source_target_pairs={{0,4},{4,8},{8,12},{12,0},{1,5},{5,9},{9,13},{13,1},{2,6},{6,10},{... | collective-permute-start | bytes 589832 | tf_op jit(solution)/shard_map/while/body/eval_jaxpr/ppermute | solution.py:12
  61.1 7.5 %collective-permute-start = (bf16[128,768]{1,0:T(8,128)(2,1)S(1)}, bf16[128,768]{1,0:T(8,128)(2,1)S(1)}, u32[]{:S(2)}, u32[]{:S(2)}) collective-permute-start(bf16[128,768]{1,0:T(8,128)(2,1)S(1)} %get-tuple-element.558), channel_id=1, source_target_pairs={{0,4},{4,8},{8,12},{12,0},{1,5},{5,9},{9,13},{13,1},{2,6},{6,10},{... | collective-permute-start | bytes 589832 | tf_op jit(solution)/shard_map/while/body/eval_jaxpr/ppermute | solution.py:12
  69.8 29.7 %copy-start.1 = (bf16[256,384]{1,0:T(8,128)(2,1)S(1)}, bf16[256,384]{1,0:T(8,128)(2,1)}, u32[]{:S(2)}) copy-start(bf16[256,384]{1,0:T(8,128)(2,1)} %param.6) | copy-start | bytes 589828
  71.0 89.8 %all-reduce.2.cloned.1.call-start = ((), (), s32[]{:S(2)}) async-start(), calls=%async_computation.4 | async-start | bytes 2359296 | tf_op jit(solution)/shard_map/psum | solution.py:103
Sparse Core Ops, SparseCore 0:
  10.8 20.1 reduce-scatter.2
  71.1 20.8 reduce-scatter.4
  101.1 59.6 all-reduce.1
where the time goes:
time: 170 us
  waiting for transfers between devices  114 us (67%)
  blocking collectives  15.7 us (9%)
  between operations  13.8 us (8%)
  other arithmetic  9.37 us (6%)
  matrix products  8.66 us (5%)
  local copies, waits for them, and re-layouts  6.9 us (4%)
  starting transfers between devices  1.78 us (1%)
    psum x1, waiting for transfers between devices, body(): head_grad = lax.psum(head_part, ('loop', 'rep'))  58.8 us
    reduce_scatter x1, waiting for transfers between devices, body(): lax.psum_scatter(grad_block.astype(jnp.bfloat16), ('enc', 'rep'), scatter...  20.9 us
    ppermute x3, waiting for transfers between devices, passed_along(): return lax.ppermute(value, axis, pairs)  17 us
    reduce_scatter x1, waiting for transfers between devices, body(): lax.psum_scatter(jnp.dot(rows, head_weight, preferred_element_type=jnp.fl...  16.8 us
    all_gather x1, blocking collectives, body(): block_feats = lax.all_gather(own_feats, ('enc', 'rep'), axis=0, tiled=True)  8.2 us
    all_gather x1, blocking collectives, body(): piece = lax.all_gather(own_grad, 'enc', axis=0, tiled=True)  7.51 us
    select_n x4, other arithmetic, tile(): piece_coef = jnp.where(piece_offsets < anchor_count, piece_coef, 0.0)  5.68 us
    unnamed x7, local copies, waits for them, and re-layouts  3.67 us
  transfers between devices with their start and end apart: 6, of which 6 were waited for; matrix products, arithmetic and copies ran while one was open for 6% of the time, Pallas kernels for 0%

commit v1 on v0

--- a/solution.py
+++ b/solution.py
@@ -100,7 +100,7 @@
         rows, piece, (((0,), (0,)), ((), ())), preferred_element_type=jnp.float32
     )
     embed_part, head_part = (embed_part, head_part)
-    head_grad = lax.psum(head_part, ("loop", "rep"))
+    head_grad = jnp.sum(lax.all_gather(head_part, ("loop", "rep")), axis=0)
     return (embed_part.astype(jnp.bfloat16), head_grad)
 
 

time: 170 us -> 209 us (1.23)
  waiting for transfers between devices: 114 us -> 145 us
  local copies, waits for them, and re-layouts: 6.9 us -> 11.5 us
  other arithmetic: 9.37 us -> 12.2 us
    all_gather x0 -> x1, waiting for transfers between devices: none -> 89.8 us  [body(): head_grad = jnp.sum(lax.all_gather(head_part, ('loop', 'rep')), axis=0)]
    psum x1 -> x0, waiting for transfers between devices: 58.8 us -> none  [body(): head_grad = lax.psum(head_part, ('loop', 'rep'))]
    unnamed x7 -> x8, local copies, waits for them, and re-layouts: 3.67 us -> 8.27 us
    reduce_sum x0 -> x1, other arithmetic: none -> 2.86 us  [body(): head_grad = jnp.sum(lax.all_gather(head_part, ('loop', 'rep')), axis=0)]
  transfers between devices with their start and end apart: 6 -> 6, of which waited for: 6 -> 6; matrix products, arithmetic and copies ran while one was open for 6% -> 5% of each run, Pallas kernels for 0% -> 0%
where the time goes in v1:
time: 209 us
  waiting for transfers between devices  145 us (69%)
  blocking collectives  15.7 us (8%)
  between operations  13.8 us (7%)
  other arithmetic  12.2 us (6%)
  local copies, waits for them, and re-layouts  11.5 us (6%)
  matrix products  8.66 us (4%)
    all_gather x1, waiting for transfers between devices, body(): head_grad = jnp.sum(lax.all_gather(head_part, ('loop', 'rep')), axis=0)  89.8 us
    reduce_scatter x1, waiting for transfers between devices, body(): lax.psum_scatter(grad_block.astype(jnp.bfloat16), ('enc', 'rep'), scatter...  20.9 us
    ppermute x3, waiting for transfers between devices, passed_along(): return lax.ppermute(value, axis, pairs)  17 us
    reduce_scatter x1, waiting for transfers between devices, body(): lax.psum_scatter(jnp.dot(rows, head_weight, preferred_element_type=jnp.fl...  16.8 us
    unnamed x8, local copies, waits for them, and re-layouts  8.27 us
    all_gather x1, blocking collectives, body(): block_feats = lax.all_gather(own_feats, ('enc', 'rep'), axis=0, tiled=True)  8.2 us
    all_gather x1, blocking collectives, body(): piece = lax.all_gather(own_grad, 'enc', axis=0, tiled=True)  7.51 us
    select_n x4, other arithmetic, tile(): piece_coef = jnp.where(piece_offsets < anchor_count, piece_coef, 0.0)  5.68 us
  transfers between devices with their start and end apart: 6, of which 6 were waited for; matrix products, arithmetic and copies ran while one was open for 5% of the time, Pallas kernels for 0%

profile of v1, /device:TPU:0, one launch (start us, length us, event | category | flops | bytes accessed | tf_op | source)
XLA Modules:
  0.0 208.5 jit_solution(9821155717590889600)
XLA Ops:
  7.2 1.0 copy-done
  8.2 2.2 %fusion.40 = f32[256,768]{1,0:T(8,128)} fusion(bf16[256,384]{1,0:T(8,128)(2,1)} %param.6, bf16[384,768]{1,0:T(8,128)(2,1)S(1)} %copy-done), kind=kOutput, calls=%fused_computation.57 | convolution fusion | flops 150994944 | bytes 1572864 | tf_op jit(solution)/shard_map/dot_general | solution.py:31
  12.0 0.8 compare_select_fusion.1
  12.8 1.5 compare_select_fusion.2
  14.2 16.8 %reduce-scatter.3.cloned.1.call-done = f32[128,768]{1,0:T(8,128)} async-done(((f32[256,768]{1,0:T(8,128)}), f32[128,768]{1,0:T(8,128)}) %reduce-scatter.3.cloned.1.call-update) | async-done | bytes 393232 | tf_op jit(solution)/shard_map/reduce_scatter | solution.py:30
  31.0 1.1 multiply_reduce_fusion.1
  32.1 8.2 %all_gather.12 = bf16[512,768]{1,0:T(8,128)(2,1)S(1)} all-gather(bf16[128,768]{1,0:T(8,128)(2,1)S(1)} %get-tuple-element.537), channel_id=1, replica_groups=mesh['groups'=2,'loop'=4,'enc'=2,'rep'=2] {'enc','rep'}, dimensions={0}, use_global_device_ids=true | all-gather | bytes 983040 | tf_op jit(solution)/shard_map/all_gather | solution.py:36
  41.5 28.3 %while.23 = (s32[]{:T(128)}, bf16[128,768]{1,0:T(8,128)(2,1)S(1)}, f32[512,768]{1,0:T(8,128)S(1)}, f32[512]{0:T(512)S(1)}, s32[]{:T(128)}, /*index=5*/s32[4]{0:T...) while((s32[]{:T(128)}, bf16[128,768]{1,0:T(8,128)(2,1)S(1)}, ...), condition=%wide.region_7.8_spmd.clone.clone, body=%wide.region_4.7_spmd.clone.clone.sunk | while | flops 203260192 | bytes 6246334 | solution.py:87
  41.5 1.5 collective-permute-start
  43.6 1.4 compare_select_fusion.4
  45.1 5.5 %collective-permute-done = bf16[128,768]{1,0:T(8,128)(2,1)S(1)} collective-permute-done((bf16[128,768]{1,0:T(8,128)(2,1)S(1)}, bf16[128,768]{1,0:T(8,128)(2,1)S(1)}, u32[]{:S(2)}, u32[]{:S(2)}) %collective-permute-start) | collective-permute-done | bytes 196640 | tf_op jit(solution)/shard_map/while/body/eval_jaxpr/ppermute | solution.py:12
  52.4 1.4 compare_select_fusion.4
  53.8 6.1 %collective-permute-done = bf16[128,768]{1,0:T(8,128)(2,1)S(1)} collective-permute-done((bf16[128,768]{1,0:T(8,128)(2,1)S(1)}, bf16[128,768]{1,0:T(8,128)(2,1)S(1)}, u32[]{:S(2)}, u32[]{:S(2)}) %collective-permute-start) | collective-permute-done | bytes 196640 | tf_op jit(solution)/shard_map/while/body/eval_jaxpr/ppermute | solution.py:12
  61.8 1.4 compare_select_fusion.4
  63.2 5.4 %collective-permute-done = bf16[128,768]{1,0:T(8,128)(2,1)S(1)} collective-permute-done((bf16[128,768]{1,0:T(8,128)(2,1)S(1)}, bf16[128,768]{1,0:T(8,128)(2,1)S(1)}, u32[]{:S(2)}, u32[]{:S(2)}) %collective-permute-start) | collective-permute-done | bytes 196640 | tf_op jit(solution)/shard_map/while/body/eval_jaxpr/ppermute | solution.py:12
  69.8 1.1 fusion.21
  71.1 20.9 %reduce-scatter.5.cloned.1.call-done = bf16[128,768]{1,0:T(8,128)(2,1)} async-done(((bf16[512,768]{1,0:T(8,128)(2,1)}), bf16[128,768]{1,0:T(8,128)(2,1)}) %reduce-scatter.5.cloned.1.call-update) | async-done | bytes 196624 | tf_op jit(solution)/shard_map/reduce_scatter | solution.py:90
  92.0 7.5 %all_gather.13 = bf16[256,768]{1,0:T(8,128)(2,1)S(1)} all-gather(bf16[128,768]{1,0:T(8,128)(2,1)} %reduce-scatter.5.cloned.1.call-done), channel_id=1, replica_groups=mesh['groups'=2,'loop'=4,'enc'=2,'rep'=2] {'enc'}, dimensions={0}, use_global_device_ids=true | all-gather | bytes 589824 | tf_op jit(solution)/shard_map/all_gather | solution.py:93
  99.5 1.4 convolution_bitcast_fusion
  100.9 1.1 convolution_convert_fusion
  102.0 89.8 %all-gather.3.cloned.1.call-done = f32[3072,768]{0,1:T(8,128)} async-done(((f32[384,768]{0,1:T(8,128)}), f32[3072,768]{0,1:T(8,128)}) %all-gather.3.cloned.1.call-update) | async-done | bytes 9437200 | tf_op jit(solution)/shard_map/all_gather | solution.py:103
  191.9 5.9 %copy.9 = f32[96,8,8,384]{3,2,1,0:T(8,128)S(1)} copy(f32[96,8,8,384]{3,1,2,0:T(8,128)} %bitcast.33) | data formatting | bytes 18874368
  197.7 2.9 %bitcast_reduce_fusion = f32[384,768]{0,1:T(8,128)S(1)} fusion(f32[96,8,8,384]{3,2,1,0:T(8,128)S(1)} %copy.9), kind=kLoop, calls=%fused_computation.23 | loop fusion | flops 2064384 | bytes 10616832 | tf_op jit(solution)/shard_map/reduce_sum | solution.py:103
  200.6 1.4 copy.8
  (39 shorter events, 8.2 us)
Async XLA Ops:
  7.2 1.1 copy-start
  7.2 3.3 %copy-start.2 = (s32[4]{0:T(128)S(1)}, s32[4]{0:T(128)}, u32[]{:S(2)}) copy-start(s32[4]{0:T(128)} %param.9) | copy-start | bytes 52
  7.2 23.8 %reduce-scatter.3.cloned.1.call-start = ((), (), s32[]{:S(2)}) async-start(), calls=%async_computation.2 | async-start | bytes 1179648 | tf_op jit(solution)/shard_map/reduce_scatter | solution.py:30
  10.4 81.6 %reduce-scatter.5.cloned.1.call-start = ((), (), s32[]{:S(2)}) async-start(), calls=%async_computation.3 | async-start | bytes 983040 | tf_op jit(solution)/shard_map/reduce_scatter | solution.py:90
  41.5 9.0 %collective-permute-start = (bf16[128,768]{1,0:T(8,128)(2,1)S(1)}, bf16[128,768]{1,0:T(8,128)(2,1)S(1)}, u32[]{:S(2)}, u32[]{:S(2)}) collective-permute-start(bf16[128,768]{1,0:T(8,128)(2,1)S(1)} %get-tuple-element.554), channel_id=1, source_target_pairs={{0,4},{4,8},{8,12},{12,0},{1,5},{5,9},{9,13},{13,1},{2,6},{6,10},{... | collective-permute-start | bytes 589832 | tf_op jit(solution)/shard_map/while/body/eval_jaxpr/ppermute | solution.py:12
  51.7 8.2 %collective-permute-start = (bf16[128,768]{1,0:T(8,128)(2,1)S(1)}, bf16[128,768]{1,0:T(8,128)(2,1)S(1)}, u32[]{:S(2)}, u32[]{:S(2)}) collective-permute-start(bf16[128,768]{1,0:T(8,128)(2,1)S(1)} %get-tuple-element.554), channel_id=1, source_target_pairs={{0,4},{4,8},{8,12},{12,0},{1,5},{5,9},{9,13},{13,1},{2,6},{6,10},{... | collective-permute-start | bytes 589832 | tf_op jit(solution)/shard_map/while/body/eval_jaxpr/ppermute | solution.py:12
  61.1 7.5 %collective-permute-start = (bf16[128,768]{1,0:T(8,128)(2,1)S(1)}, bf16[128,768]{1,0:T(8,128)(2,1)S(1)}, u32[]{:S(2)}, u32[]{:S(2)}) collective-permute-start(bf16[128,768]{1,0:T(8,128)(2,1)S(1)} %get-tuple-element.554), channel_id=1, source_target_pairs={{0,4},{4,8},{8,12},{12,0},{1,5},{5,9},{9,13},{13,1},{2,6},{6,10},{... | collective-permute-start | bytes 589832 | tf_op jit(solution)/shard_map/while/body/eval_jaxpr/ppermute | solution.py:12
  69.8 29.7 %copy-start.1 = (bf16[256,384]{1,0:T(8,128)(2,1)S(1)}, bf16[256,384]{1,0:T(8,128)(2,1)}, u32[]{:S(2)}) copy-start(bf16[256,384]{1,0:T(8,128)(2,1)} %param.6) | copy-start | bytes 589828
  71.0 120.9 %all-gather.3.cloned.1.call-start = ((), (), s32[]{:S(2)}) async-start(), calls=%async_computation.4 | async-start | bytes 10616832 | tf_op jit(solution)/shard_map/all_gather | solution.py:103
Sparse Core Ops, SparseCore 0:
  10.8 20.1 reduce-scatter.2
  71.1 20.8 reduce-scatter.4
  101.1 90.7 all-gather.2
